TPU v7x, 32 devices: a whole 2x2x4 slice. The times are simulated.
32 devices in a mesh: dp: 2 (over y), row: 2 (over core), col: 8 (over z, x).
Axes of the slice: x: 2, y: 2, z: 4, core: 2. Of those that a mesh axis runs over, the one named last changes fastest.
Arguments:
- activations: bfloat16 [2048, 16384], P(('dp', 'row'), 'col'), may hold values from -6 to 6
- cotangent: bfloat16 [2048, 16384], P(('dp', 'row'), 'col'), may hold values from -6 to 6
- gate_saved: bfloat16 [2048, 6656], P(('dp', 'col'), 'row'), may hold values from -6 to 6
- up_saved: bfloat16 [2048, 6656], P(('dp', 'col'), 'row'), may hold values from -6 to 6
- w_gate: bfloat16 [16384, 6656], P('col', 'row'), may hold values from -0.046875 to 0.046875
- w_up: bfloat16 [16384, 6656], P('col', 'row'), may hold values from -0.046875 to 0.046875
- w_down: bfloat16 [6656, 16384], P('row', 'col'), may hold values from -0.078125 to 0.078125
- assignment: int32 [4], replicated, may hold values from 0 to 3, each once
- pair_lengths: int32 [8], replicated, may hold values from 1 to 256, 1536 in all
Outputs:
- input_grad: bfloat16 [2048, 16384], P(('dp', 'row'), 'col')
- gate_grad: bfloat16 [16384, 6656], P(('col', 'dp'), 'row')
- up_grad: bfloat16 [16384, 6656], P(('col', 'dp'), 'row')
- down_grad: bfloat16 [6656, 16384], P(('row', 'dp'), 'col')
Inputs may be any that keep to these rules, and one draw needn't show every extreme that they name: `assignment`: each of the 4 pairs stands in exactly one pair slot; pair slot s belongs to batch s // 2. `pair_lengths`: entry 2 p is the live length of pair p's chosen sequence and entry 2 p + 1 that of its rejected one; the largest entry is exactly 256.
All inputs are finite; a program needn't handle non-finite values.
Results may differ from a plain program's by a relative error of at most 0.019.
Values may be sent and summed in bfloat16 or wider, within the bound.
A program may use at most 192 MiB of HBM per device.

v0:
```python
import jax
import jax.numpy as jnp
from jax import lax
from jax.sharding import PartitionSpec as P

SEQ = 256


def contract_last(left, right):
    return lax.dot_general(
        left, right, (((1,), (1,)), ((), ())), preferred_element_type=jnp.float32
    )


def contract_first(left, right):
    return lax.dot_general(
        left, right, (((0,), (0,)), ((), ())), preferred_element_type=jnp.float32
    )


def live_mask(assignment, pair_lengths, batch_id, row_count):
    seq_count = row_count // SEQ
    seq_index = jnp.arange(seq_count, dtype=jnp.int32)
    slot_ids = batch_id * (seq_count // 2) + seq_index // 2
    slot_table = jnp.arange(assignment.shape[0], dtype=jnp.int32)
    pair_ids = jnp.sum(
        jnp.where(slot_table[None, :] == slot_ids[:, None], assignment[None, :], 0), axis=1
    )
    entry_ids = 2 * pair_ids + seq_index % 2
    entry_table = jnp.arange(pair_lengths.shape[0], dtype=jnp.int32)
    live_len = jnp.sum(
        jnp.where(entry_table[None, :] == entry_ids[:, None], pair_lengths[None, :], 0), axis=1
    )
    position = jnp.arange(row_count, dtype=jnp.int32)
    return position % SEQ < jnp.repeat(live_len, SEQ, total_repeat_length=row_count)


def swiglu_grads(head_grad, gate_vals, up_vals):
    gate_float = gate_vals.astype(jnp.float32)
    up_float = up_vals.astype(jnp.float32)
    sigmoid_gate = jax.nn.sigmoid(gate_float)
    silu_gate = gate_float * sigmoid_gate
    hidden = (silu_gate * up_float).astype(jnp.bfloat16)
    grad_gate = (
        head_grad * up_float * sigmoid_gate * (1.0 + gate_float * (1.0 - sigmoid_gate))
    ).astype(jnp.bfloat16)
    grad_up = (head_grad * silu_gate).astype(jnp.bfloat16)
    return (grad_gate, grad_up, hidden)


def on_device(
    activations, cotangent, gate_saved, up_saved, w_gate, w_up, w_down, assignment, pair_lengths
):
    input_rows, output_grads = (
        lax.all_gather(activations, "row", axis=0, tiled=True),
        lax.all_gather(cotangent, "row", axis=0, tiled=True),
    )
    row_count = input_rows.shape[0]
    batch_id = lax.axis_index("dp")
    live_tokens = live_mask(assignment, pair_lengths, batch_id, row_count)
    masked = jnp.where(live_tokens[:, None], output_grads, jnp.zeros_like(output_grads))
    head_grad = lax.psum(contract_last(masked, w_down).astype(jnp.bfloat16), "col").astype(
        jnp.float32
    )
    gate_rows, up_rows = (
        lax.all_gather(gate_saved, "col", axis=0, tiled=True),
        lax.all_gather(up_saved, "col", axis=0, tiled=True),
    )
    grad_gate, grad_up, hidden = swiglu_grads(head_grad, gate_rows, up_rows)
    input_count = row_count // lax.axis_size("row")
    left_gate = lax.slice_in_dim(grad_gate, 0, input_count * lax.axis_size("row"), axis=0)
    left_up = lax.slice_in_dim(grad_up, 0, input_count * lax.axis_size("row"), axis=0)
    input_grad = lax.psum_scatter(
        (contract_last(left_gate, w_gate) + contract_last(left_up, w_up)).astype(jnp.bfloat16),
        "row",
        scatter_dimension=0,
        tiled=True,
    )
    grad_scale = 1.0 / jnp.sqrt(jnp.float32(row_count * lax.axis_size("dp")))
    gate_term = contract_first(input_rows, grad_gate) * grad_scale
    up_term = contract_first(input_rows, grad_up) * grad_scale
    down_term = contract_first(hidden, masked) * grad_scale
    gate_total, up_total, down_total = (
        lax.psum_scatter(
            gate_term.astype(jnp.bfloat16), "dp", scatter_dimension=0, tiled=True
        ).astype(jnp.float32),
        lax.psum_scatter(
            up_term.astype(jnp.bfloat16), "dp", scatter_dimension=0, tiled=True
        ).astype(jnp.float32),
        lax.psum_scatter(
            down_term.astype(jnp.bfloat16), "dp", scatter_dimension=0, tiled=True
        ).astype(jnp.float32),
    )
    return (
        input_grad,
        gate_total.astype(jnp.bfloat16),
        up_total.astype(jnp.bfloat16),
        down_total.astype(jnp.bfloat16),
    )


def solution(mesh):
    return jax.shard_map(
        on_device,
        mesh=mesh,
        in_specs=(
            P(("dp", "row"), "col"),
            P(("dp", "row"), "col"),
            P(("dp", "col"), "row"),
            P(("dp", "col"), "row"),
            P("col", "row"),
            P("col", "row"),
            P("row", "col"),
            P(),
            P(),
        ),
        out_specs=(
            P(("dp", "row"), "col"),
            P(("col", "dp"), "row"),
            P(("col", "dp"), "row"),
            P(("row", "dp"), "col"),
        ),
        check_vma=False,
    )
```

profile of v0, /device:TPU:0, one launch (start us, length us, event | category | flops | bytes accessed | tf_op | source)
XLA Modules:
  0.0 984.8 jit_solution(13904595718828324722)
XLA Ops:
  7.2 0.0 all-gather.5.cloned.1.call-start
  7.2 0.7 all-gather.5.cloned.1.call-update
  7.9 0.0 all-gather.11.cloned.1.call-start
  7.9 0.7 all-gather.11.cloned.1.call-update
  8.6 0.0 all-reduce.2.cloned.1.call-start
  8.7 0.8 select_reduce_fusion.1
  9.6 0.8 select_reduce_fusion
  10.4 0.6 fusion.23
  11.0 3.3 fusion.12
  14.3 0.0 copy-start.1
  14.3 11.7 %all-gather.5.cloned.1.call-done = bf16[1024,2048]{1,0:T(8,128)(2,1)} async-done(((bf16[512,2048]{1,0:T(8,128)(2,1)}), bf16[1024,2048]{1,0:T(8,128)(2,1)}) %all-gather.5.cloned.1.call-update) | async-done | bytes 4194320 | tf_op jit(solution)/shard_map/all_gather | solution.py:56
  26.0 21.6 %convolution_convert_fusion = bf16[1024,3328]{1,0:T(8,128)(2,1)} fusion(bf16[3328,2048]{1,0:T(8,128)(2,1)} %param.17, bf16[1024,2048]{1,0:T(8,128)(2,1)} %all-gather.5.cloned.1.call-done, pred[1024]{0:T(1024)(128)(4,1)S(1)} %fusion.12), kind=kOutput, calls=%fused_computation.21 | convolution fusion | flops 13964148736 | bytes 24642560 | tf_op jit(solution)/shard_map/dot_general | solution.py:10
  47.5 0.0 copy-done.1
  47.5 0.0 all-reduce.2.cloned.1.call-update
  47.6 0.0 all-gather.9.cloned.1.call-start
  47.6 0.5 all-gather.9.cloned.1.call-update
  48.2 0.0 all-gather.7.cloned.1.call-start
  48.2 0.5 all-gather.7.cloned.1.call-update
  48.7 0.2 reduce-scatter.9.cloned.1.call-start
  49.0 0.0 all-gather.11.cloned.1.call-done
  49.0 227.5 %all-reduce.2.cloned.1.call-done = bf16[1024,3328]{1,0:T(8,128)(2,1)} async-done(((bf16[1024,3328]{1,0:T(8,128)(2,1)}), bf16[1024,3328]{1,0:T(8,128)(2,1)}) %all-reduce.2.cloned.1.call-update) | async-done | bytes 6815760 | tf_op jit(solution)/shard_map/psum | solution.py:62
  276.4 106.8 %all-gather.9.cloned.1.call-done = bf16[1024,3328]{1,0:T(8,128)(2,1)} async-done(((bf16[128,3328]{1,0:T(8,128)(2,1)}), bf16[1024,3328]{1,0:T(8,128)(2,1)}) %all-gather.9.cloned.1.call-update) | async-done | bytes 6815760 | tf_op jit(solution)/shard_map/all_gather | solution.py:66
  383.2 23.4 %fusion.10 = bf16[2048,3328]{0,1:T(8,128)(2,1)} fusion(bf16[1024,2048]{1,0:T(8,128)(2,1)} %all-gather.11.cloned.1.call-done, bf16[1024,3328]{1,0:T(8,128)(2,1)} %all-reduce.2.cloned.1.call-done, bf16[1024,3328]{1,0:T(8,128)(2,1)} %all-gather.9.cloned.1.call-done), kind=kOutput, calls=%fused_computation.19 | convolution fusion | flops 13999538176 | bytes 31457280 | tf_op jit(solution)/shard_map/dot_general | solution.py:16
  406.6 0.0 reduce-scatter.9.cloned.1.call-update
  406.7 0.3 reduce-scatter.7.cloned.1.call-start
  406.9 82.1 %all-gather.7.cloned.1.call-done = bf16[1024,3328]{1,0:T(8,128)(2,1)} async-done(((bf16[128,3328]{1,0:T(8,128)(2,1)}), bf16[1024,3328]{1,0:T(8,128)(2,1)}) %all-gather.7.cloned.1.call-update) | async-done | bytes 6815760 | tf_op jit(solution)/shard_map/all_gather | solution.py:67
  489.0 0.0 copy-start.3
  489.0 11.0 %fusion.3 = bf16[1024,3328]{1,0:T(8,128)(2,1)S(1)} fusion(bf16[1024,3328]{1,0:T(8,128)(2,1)} %all-gather.7.cloned.1.call-done, bf16[1024,3328]{1,0:T(8,128)(2,1)} %all-reduce.2.cloned.1.call-done, bf16[1024,3328]{1,0:T(8,128)(2,1)} %all-gather.9.cloned.1.call-done), kind=kLoop, calls=%fused_computation.12 | loop fusion | flops 44302336 | bytes 27262976 | tf_op jit(solution)/shard_map/convert_element_type | solution.py:46
  500.0 0.0 copy-start
  500.0 2.9 copy-done
  502.9 0.0 copy-done.3
  502.9 17.0 %fusion.9 = bf16[2048,3328]{0,1:T(8,128)(2,1)} fusion(bf16[1024,3328]{1,0:T(8,128)(2,1)S(1)} %fusion.3, bf16[1024,2048]{1,0:T(8,128)(2,1)S(1)} %copy-done.3), kind=kOutput, calls=%fused_computation.18 | convolution fusion | flops 13972275200 | bytes 24641536 | tf_op jit(solution)/shard_map/dot_general | solution.py:16
  519.9 0.0 reduce-scatter.7.cloned.1.call-update
  519.9 0.0 reduce-scatter.5.cloned.1.call-start
  520.0 20.2 %fusion.24 = f32[1024,2048]{1,0:T(8,128)} fusion(bf16[1024,3328]{1,0:T(8,128)(2,1)} %copy-done, bf16[2048,3328]{1,0:T(8,128)(2,1)} %param.15), kind=kOutput, calls=%fused_computation.44 | convolution fusion | flops 13958643712 | bytes 28835840 | tf_op jit(solution)/shard_map/dot_general | solution.py:10
  540.1 0.0 copy-start.2
  540.1 24.5 %add_convert_fusion = bf16[1024,2048]{1,0:T(8,128)(2,1)} fusion(f32[1024,2048]{1,0:T(8,128)} %fusion.24, bf16[2048,3328]{1,0:T(8,128)(2,1)} %param.16, bf16[1024,3328]{1,0:T(8,128)(2,1)} %all-reduce.2.cloned.1.call-done, bf16[1024,3328]{1,0:T(8,128)(2,1)} %all-gather.9.cloned.1.call-done), kind=kOutput, calls=%fused_computation.20 | convolution fusion | flops 13990100992 | bytes 39845888 | tf_op jit(solution)/shard_map/dot_general | solution.py:10
  564.6 0.0 reduce-scatter.5.cloned.1.call-update
  564.7 0.3 reduce-scatter.11.cloned.1.call-start
  565.0 0.0 copy-done.2
  565.0 28.9 %multiply_convert_fusion = bf16[3328,2048]{1,0:T(8,128)(2,1)} fusion(bf16[1024,3328]{1,0:T(8,128)(2,1)} %all-gather.7.cloned.1.call-done, bf16[1024,3328]{1,0:T(8,128)(2,1)} %all-gather.9.cloned.1.call-done, bf16[1024,2048]{1,0:T(8,128)(2,1)} %all-gather.5.cloned.1.call-done, pred[1024]{0:T(1024)(128)(4,1)S(1)} %copy-done.2), kind=kOutput, calls=%fused_computation | convolution fusion | flops 14001635328 | bytes 31458304 | tf_op jit(solution)/shard_map/dot_general | solution.py:16
  593.8 0.0 reduce-scatter.11.cloned.1.call-update
  593.8 51.3 %reduce-scatter.9.cloned.1.call-done = bf16[1024,3328]{0,1:T(8,128)(2,1)} async-done(((bf16[2048,3328]{0,1:T(8,128)(2,1)}), bf16[1024,3328]{0,1:T(8,128)(2,1)}) %reduce-scatter.9.cloned.1.call-update) | async-done | bytes 6815760 | tf_op jit(solution)/shard_map/reduce_scatter | solution.py:87
  645.2 9.9 %copy.16 = bf16[1024,3328]{1,0:T(8,128)(2,1)} copy(bf16[1024,3328]{0,1:T(8,128)(2,1)} %reduce-scatter.9.cloned.1.call-done) | data formatting | bytes 13631488
  655.1 148.2 %reduce-scatter.7.cloned.1.call-done = bf16[1024,3328]{0,1:T(8,128)(2,1)} async-done(((bf16[2048,3328]{0,1:T(8,128)(2,1)}), bf16[1024,3328]{0,1:T(8,128)(2,1)}) %reduce-scatter.7.cloned.1.call-update) | async-done | bytes 6815760 | tf_op jit(solution)/shard_map/reduce_scatter | solution.py:84
  803.3 9.9 %copy.15 = bf16[1024,3328]{1,0:T(8,128)(2,1)} copy(bf16[1024,3328]{0,1:T(8,128)(2,1)} %reduce-scatter.7.cloned.1.call-done) | data formatting | bytes 13631488
  813.2 5.0 reduce-scatter.5.cloned.1.call-done
  818.2 160.1 %reduce-scatter.11.cloned.1.call-done = bf16[1664,2048]{1,0:T(8,128)(2,1)} async-done(((bf16[3328,2048]{1,0:T(8,128)(2,1)}), bf16[1664,2048]{1,0:T(8,128)(2,1)}) %reduce-scatter.11.cloned.1.call-update) | async-done | bytes 6815760 | tf_op jit(solution)/shard_map/reduce_scatter | solution.py:90
  (2 shorter events, 0.0 us)
Async XLA Ops:
  7.2 18.8 %all-gather.5.cloned.1.call-start = ((), (), s32[]{:S(2)}) async-start(), calls=%async_computation.4 | async-start | bytes 6291456 | tf_op jit(solution)/shard_map/all_gather | solution.py:56
  7.9 41.1 %all-gather.11.cloned.1.call-start = ((), (), s32[]{:S(2)}) async-start(), calls=%async_computation.9 | async-start | bytes 6291456 | tf_op jit(solution)/shard_map/all_gather | solution.py:55
  8.6 267.8 %all-reduce.2.cloned.1.call-start = ((), (), s32[]{:S(2)}) async-start(), calls=%async_computation.5 | async-start | bytes 13631488 | tf_op jit(solution)/shard_map/psum | solution.py:62
  14.3 33.2 %copy-start.1 = (pred[1024]{0:T(1024)(128)(4,1)}, pred[1024]{0:T(1024)(128)(4,1)S(1)}, u32[]{:S(2)}) copy-start(pred[1024]{0:T(1024)(128)(4,1)S(1)} %fusion.12) | copy-start | bytes 3076
  47.6 335.6 %all-gather.9.cloned.1.call-start = ((), (), s32[]{:S(2)}) async-start(), calls=%async_computation.7 | async-start | bytes 7667712 | tf_op jit(solution)/shard_map/all_gather | solution.py:66
  48.2 440.9 %all-gather.7.cloned.1.call-start = ((), (), s32[]{:S(2)}) async-start(), calls=%async_computation.6 | async-start | bytes 7667712 | tf_op jit(solution)/shard_map/all_gather | solution.py:67
  48.7 596.4 %reduce-scatter.9.cloned.1.call-start = ((), (), s32[]{:S(2)}) async-start(), calls=%async_computation.11 | async-start | bytes 20447232 | tf_op jit(solution)/shard_map/reduce_scatter | solution.py:87
  406.7 396.6 %reduce-scatter.7.cloned.1.call-start = ((), (), s32[]{:S(2)}) async-start(), calls=%async_computation.10 | async-start | bytes 20447232 | tf_op jit(solution)/shard_map/reduce_scatter | solution.py:84
  489.0 13.9 %copy-start.3 = (bf16[1024,2048]{1,0:T(8,128)(2,1)S(1)}, bf16[1024,2048]{1,0:T(8,128)(2,1)}, u32[]{:S(2)}) copy-start(bf16[1024,2048]{1,0:T(8,128)(2,1)} %all-gather.11.cloned.1.call-done) | copy-start | bytes 12582916
  500.0 2.9 copy-start
  519.9 298.3 %reduce-scatter.5.cloned.1.call-start = ((), (), s32[]{:S(2)}) async-start(), calls=%async_computation.8 | async-start | bytes 6291456 | tf_op jit(solution)/shard_map/reduce_scatter | solution.py:73
  540.1 24.8 %copy-start.2 = (pred[1024]{0:T(1024)(128)(4,1)S(1)}, pred[1024]{0:T(1024)(128)(4,1)}, u32[]{:S(2)}) copy-start(pred[1024]{0:T(1024)(128)(4,1)} %copy-done.1) | copy-start | bytes 3076
  564.7 413.7 %reduce-scatter.11.cloned.1.call-start = ((), (), s32[]{:S(2)}) async-start(), calls=%async_computation.12 | async-start | bytes 20447232 | tf_op jit(solution)/shard_map/reduce_scatter | solution.py:90
Sparse Core Ops, SparseCore 0:
  9.5 16.3 all-gather.4
  27.5 14.8 all-gather.10
  47.7 228.7 all-reduce.1
  278.5 104.6 all-gather.8
  385.2 103.7 all-gather.6
  491.2 153.9 reduce-scatter.8
  647.5 155.7 reduce-scatter.6
  806.2 12.0 reduce-scatter.4
  821.2 157.0 reduce-scatter.10
where the time goes:
time: 985 us
  waiting for transfers between devices  795 us (81%)
  matrix products  136 us (14%)
  local copies, waits for them, and re-layouts  23.3 us (2%)
  other arithmetic  16 us (2%)
  between operations  13.9 us (1%)
    psum x1, waiting for transfers between devices, on_device(): lax.psum(contract_last(masked, w_down).astype(jnp.bfloat16), 'col')  227 us
    reduce_scatter x1, waiting for transfers between devices, on_device(): lax.psum_scatter(down_term.astype(jnp.bfloat16), 'dp', scatter_dimension=...  160 us
    reduce_scatter x1, waiting for transfers between devices, on_device(): lax.psum_scatter(gate_term.astype(jnp.bfloat16), 'dp', scatter_dimension=...  148 us
    all_gather x1, waiting for transfers between devices, on_device(): lax.all_gather(gate_saved, 'col', axis=0, tiled=True)  107 us
    all_gather x1, waiting for transfers between devices, on_device(): lax.all_gather(up_saved, 'col', axis=0, tiled=True)  82.1 us
    dot_general x3, matrix products, contract_first(): lax.dot_general(left, right, (((0,), (0,)), ((), ())), preferred_element_...  69.3 us
    dot_general x3, matrix products, contract_last(): lax.dot_general(left, right, (((1,), (1,)), ((), ())), preferred_element_...  66.2 us
    reduce_scatter x1, waiting for transfers between devices, on_device(): lax.psum_scatter(up_term.astype(jnp.bfloat16), 'dp', scatter_dimension=0,...  51.3 us
  transfers between devices with their start and end apart: 9, of which 8 were waited for; matrix products, arithmetic and copies ran while one was open for 17% of the time, Pallas kernels for 0%

commit v1 on v0

v1 whole, which is shorter than its diff:
```python
import jax
import jax.numpy as jnp
from jax import lax
from jax.sharding import PartitionSpec as P

SEQ = 256
SHARES = (2, 3, 4, 4)


def contract_last(left, right):
    return lax.dot_general(
        left, right, (((1,), (1,)), ((), ())), preferred_element_type=jnp.float32
    )


def contract_first(left, right):
    return lax.dot_general(
        left, right, (((0,), (0,)), ((), ())), preferred_element_type=jnp.float32
    )


def cuts_of(size):
    whole = sum(SHARES)
    marks = [size * sum(SHARES[:i]) // whole for i in range(len(SHARES) + 1)]
    return list(zip(marks[:-1], marks[1:]))


def after(value, earlier):
    value, earlier = lax.optimization_barrier((value, earlier))
    return value, earlier


def placed(whole, piece, start):
    return lax.dynamic_update_slice_in_dim(whole, piece, start, 1)


def shifted(value, axis, shift):
    count = lax.axis_size(axis)
    return lax.ppermute(value, axis, [(i, (i + shift) % count) for i in range(count)])


def gather_rows(block, axis):
    count = lax.axis_size(axis)
    me = lax.axis_index(axis)
    rows = block.shape[0]
    whole = jnp.zeros((rows * count,) + block.shape[1:], block.dtype)
    whole = lax.dynamic_update_slice_in_dim(whole, block, me * rows, 0)
    for shift in range(1, count):
        source = (me - shift + count) % count
        whole = lax.dynamic_update_slice_in_dim(
            whole, shifted(block, axis, shift), source * rows, 0
        )
    return whole


def live_rows(assignment, pair_lengths, first, row_count):
    token = first + jnp.arange(row_count, dtype=jnp.int32)
    slot_table = jnp.arange(assignment.shape[0], dtype=jnp.int32)
    pair_ids = jnp.sum(
        jnp.where(slot_table[None, :] == (token // (2 * SEQ))[:, None], assignment[None, :], 0),
        axis=1,
    )
    entry_ids = 2 * pair_ids + token // SEQ % 2
    entry_table = jnp.arange(pair_lengths.shape[0], dtype=jnp.int32)
    live_len = jnp.sum(
        jnp.where(entry_table[None, :] == entry_ids[:, None], pair_lengths[None, :], 0), axis=1
    )
    return (token % SEQ < live_len)[:, None]


def on_device(
    activations, cotangent, gate_saved, up_saved, w_gate, w_up, w_down, assignment, pair_lengths
):
    dp_count, row_size, col_count = (
        lax.axis_size("dp"), lax.axis_size("row"), lax.axis_size("col"))
    dp, row, col = lax.axis_index("dp"), lax.axis_index("row"), lax.axis_index("col")
    bf16 = jnp.bfloat16
    shard_rows, ff = gate_saved.shape
    width = activations.shape[1]
    batch_rows = shard_rows * col_count
    scale = 1.0 / jnp.sqrt(jnp.float32(batch_rows * dp_count))
    live = live_rows(assignment, pair_lengths, (dp * col_count + col) * shard_rows, shard_rows)

    gate_float = gate_saved.astype(jnp.float32)
    up_float = up_saved.astype(jnp.float32)
    sig = jax.nn.sigmoid(gate_float)
    silu = gate_float * sig
    hidden = jnp.where(live, (silu * up_float), 0.0).astype(bf16)

    grads_batch = gather_rows(cotangent, "row")
    inputs_batch = gather_rows(activations, "row")

    half_ff = ff // dp_count
    hidden_parts = [lax.dynamic_slice_in_dim(hidden, dp * half_ff, half_ff, 1)]
    grads_all = [grads_batch]
    for shift in range(1, dp_count):
        target = (dp + shift) % dp_count
        hidden_parts.append(
            shifted(lax.dynamic_slice_in_dim(hidden, target * half_ff, half_ff, 1), "dp", shift)
        )
        grads_all.append(gather_rows(shifted(cotangent, "dp", shift), "row"))

    half_width = width // dp_count
    own_inputs = lax.dynamic_slice_in_dim(inputs_batch, dp * half_width, half_width, 1)
    far_inputs = [
        lax.dynamic_slice_in_dim(
            inputs_batch, ((dp + shift) % dp_count) * half_width, half_width, 1
        )
        for shift in range(1, dp_count)
    ]

    term = contract_last(grads_batch, w_down).astype(bf16)
    head = lax.psum_scatter(term, "col", scatter_dimension=0, tiled=True).astype(jnp.float32)
    head = jnp.where(live, head, 0.0)
    grad_gate = (head * up_float * sig * (1.0 + gate_float * (1.0 - sig))).astype(bf16)
    grad_up = (head * silu).astype(bf16)

    input_sum = None
    chunks = cuts_of(ff)
    gathered, far_terms, far_parts = [], [], []

    def send(index):
        far_parts[index:] = [
            [shifted(term, "dp", shift) for shift, term in enumerate(far_terms[index], 1)]
        ]

    for index, (low, high) in enumerate(chunks):
        pair = jnp.concatenate([grad_gate[:, low:high], grad_up[:, low:high]], axis=1)
        if index == 0:
            pair, (grads_all[1:], hidden_parts[1:], own_inputs, far_inputs) = after(
                pair, (grads_all[1:], hidden_parts[1:], own_inputs, far_inputs)
            )
        elif index == 1:
            pair, gathered[0] = after(pair, gathered[0])
        else:
            if index + 1 == len(chunks):
                pair, far_terms[-1] = after(pair, far_terms[-1])
                send(index - 1)
            pair, (gathered[-1], far_parts[index - 2]) = after(
                pair, (gathered[-1], far_parts[index - 2])
            )
        both = lax.all_gather(pair, "col", axis=0, tiled=True)
        gathered.append(both)
        far_terms.append(None)
        far_parts.append(None)
        far_terms[index] = [(contract_first(far, both) * scale).astype(bf16) for far in far_inputs]
        send(index)
    hidden_pair, gathered[-1] = after(jnp.concatenate(hidden_parts, axis=1), gathered[-1])
    far_terms[-1], far_parts[-2] = after(far_terms[-1], far_parts[-2])
    send(len(chunks) - 1)
    hidden_rows = lax.all_gather(hidden_pair, "col", axis=0, tiled=True)

    gate_grad = jnp.zeros((half_width, ff), bf16)
    up_grad = jnp.zeros((half_width, ff), bf16)
    for (low, high), both, parts in zip(chunks, gathered, far_parts):
        size = high - low
        gate_total = (contract_first(own_inputs, both[:, :size]) * scale).astype(bf16)
        up_total = (contract_first(own_inputs, both[:, size:]) * scale).astype(bf16)
        gate_total = gate_total.astype(jnp.float32)
        up_total = up_total.astype(jnp.float32)
        for part in parts:
            gate_total = gate_total + part[:, :size].astype(jnp.float32)
            up_total = up_total + part[:, size:].astype(jnp.float32)
        gate_grad = placed(gate_grad, gate_total.astype(bf16), low)
        up_grad = placed(up_grad, up_total.astype(bf16), low)
        piece = contract_last(both[:, :size], w_gate[:, low:high]) + contract_last(
            both[:, size:], w_up[:, low:high]
        )
        input_sum = piece if input_sum is None else input_sum + piece

    input_term = input_sum.astype(bf16)
    own_rows = activations.shape[0]
    input_grad = lax.dynamic_slice_in_dim(input_term, row * own_rows, own_rows, 0).astype(
        jnp.float32
    )
    for shift in range(1, row_size):
        target = (row + shift) % row_size
        part = lax.dynamic_slice_in_dim(input_term, target * own_rows, own_rows, 0)
        input_grad = input_grad + shifted(part, "row", shift).astype(jnp.float32)

    down = None
    for index, grads in enumerate(grads_all):
        rows = hidden_rows[:, index * half_ff : (index + 1) * half_ff]
        piece = (contract_first(rows, grads) * scale).astype(bf16).astype(jnp.float32)
        down = piece if down is None else down + piece

    return (
        input_grad.astype(bf16),
        gate_grad,
        up_grad,
        down.astype(bf16),
    )


def solution(mesh):
    return jax.shard_map(
        on_device,
        mesh=mesh,
        in_specs=(
            P(("dp", "row"), "col"),
            P(("dp", "row"), "col"),
            P(("dp", "col"), "row"),
            P(("dp", "col"), "row"),
            P("col", "row"),
            P("col", "row"),
            P("row", "col"),
            P(),
            P(),
        ),
        out_specs=(
            P(("dp", "row"), "col"),
            P(("col", "dp"), "row"),
            P(("col", "dp"), "row"),
            P(("row", "dp"), "col"),
        ),
        check_vma=False,
    )
```

time: 985 us -> 619 us (0.63)
  waiting for transfers between devices: 795 us -> 348 us
  matrix products: 136 us -> 190 us
  local copies, waits for them, and re-layouts: 23.3 us -> 36.7 us
  starting transfers between devices: 1.02 us -> 11.6 us
    reduce_scatter x4 -> x1, waiting for transfers between devices: 365 us -> 69.9 us  [on_device(): lax.psum_scatter(term, 'col', scatter_dimension=0, tiled=True)]
    psum x1 -> x0, waiting for transfers between devices: 227 us -> none  [on_device(): lax.psum(contract_last(masked, w_down).astype(jnp.bfloat16), 'col')]
    ppermute x0 -> x10, waiting for transfers between devices: none -> 121 us  [shifted(): lax.ppermute(value, axis, [(i, (i + shift) % count) for i in range(count)])]
    all_gather x4 -> x5, waiting for transfers between devices: 201 us -> 158 us  [the longest x4 158 us: on_device(): both = lax.all_gather(pair, 'col', axis=0, tiled=True)]
    dot_general x3 -> x9, matrix products: 66.2 us -> 103 us  [contract_last(): lax.dot_general(left, right, (((1,), (1,)), ((), ())), preferred_element_...]
    dynamic_update_slice x0 -> x8, local copies, waits for them, and re-layouts: none -> 20.5 us  [the longest x3 8.18 us: gather_rows(): lax.dynamic_update_slice_in_dim(whole, shifted(block, axis, shift), sourc...]
    unnamed x10 -> x38, local copies, waits for them, and re-layouts: 22.7 us -> 3.83 us
    dot_general x3 -> x14, matrix products: 69.3 us -> 87.7 us  [contract_first(): lax.dot_general(left, right, (((0,), (0,)), ((), ())), preferred_element_...]
  transfers between devices with their start and end apart: 9 -> 16, of which waited for: 8 -> 11; matrix products, arithmetic and copies ran while one was open for 17% -> 31% of each run, Pallas kernels for 0% -> 0%
where the time goes in v1:
time: 619 us; the launch traced here: 611 us
  waiting for transfers between devices  348 us (56%)
  matrix products  190 us (31%)
  local copies, waits for them, and re-layouts  36.7 us (6%)
  between operations  14.7 us (2%)
  starting transfers between devices  11.6 us (2%)
  other arithmetic  8.78 us (1%)
    all_gather x4, waiting for transfers between devices, on_device(): both = lax.all_gather(pair, 'col', axis=0, tiled=True)  158 us
    ppermute x10, waiting for transfers between devices, shifted(): lax.ppermute(value, axis, [(i, (i + shift) % count) for i in range(count)])  121 us
    dot_general x9, matrix products, contract_last(): lax.dot_general(left, right, (((1,), (1,)), ((), ())), preferred_element_...  103 us
    dot_general x14, matrix products, contract_first(): lax.dot_general(left, right, (((0,), (0,)), ((), ())), preferred_element_...  87.7 us
    reduce_scatter x1, waiting for transfers between devices, on_device(): lax.psum_scatter(term, 'col', scatter_dimension=0, tiled=True)  69.9 us
  transfers between devices with their start and end apart: 16, of which 11 were waited for; matrix products, arithmetic and copies ran while one was open for 31% of the time, Pallas kernels for 0%

profile of v1, /device:TPU:0, one launch (start us, length us, event | category | flops | bytes accessed | tf_op | source)
XLA Modules:
  0.0 610.5 jit_solution(16082898172025559969)
XLA Ops:
  7.2 0.5 collective-permute-start
  7.7 0.5 broadcast.154.clone
  8.3 0.5 copy-done.5
  9.1 2.8 collective-permute-done
  11.9 1.8 constant_dynamic-update-slice_fusion.4
  13.7 2.0 copy-done.1
  15.7 20.2 %convolution_convert_fusion = bf16[1024,3328]{1,0:T(8,128)(2,1)} fusion(bf16[1024,2048]{1,0:T(8,128)(2,1)S(1)} %constant_dynamic-update-slice_fusion.4, bf16[3328,2048]{1,0:T(8,128)(2,1)} %param.15), kind=kOutput, calls=%fused_computation.6 | convolution fusion | flops 13962051584 | bytes 24641536 | tf_op jit(solution)/shard_map/dot_general | solution.py:11
  36.0 3.0 collective-permute-start.1
  39.2 2.5 broadcast.154.clone.2
  41.7 1.5 constant_dynamic-update-slice_fusion.1
  43.2 41.8 %collective-permute-done.1 = bf16[512,2048]{1,0:T(8,128)(2,1)} collective-permute-done((bf16[512,2048]{1,0:T(8,128)(2,1)S(1)}, bf16[512,2048]{1,0:T(8,128)(2,1)}, u32[]{:S(2)}, u32[]{:S(2)}) %collective-permute-start.1) | collective-permute-done | bytes 2097184 | tf_op jit(solution)/shard_map/ppermute | solution.py:39
  85.0 2.5 broadcast.154.clone.1
  87.6 3.4 constant_dynamic-update-slice_fusion.3
  90.9 3.2 constant_dynamic-update-slice_fusion
  94.1 69.9 %reduce-scatter.2.cloned.1.call-done = bf16[128,3328]{1,0:T(8,128)(2,1)} async-done(((bf16[1024,3328]{1,0:T(8,128)(2,1)}), bf16[128,3328]{1,0:T(8,128)(2,1)}) %reduce-scatter.2.cloned.1.call-update) | async-done | bytes 851984 | tf_op jit(solution)/shard_map/reduce_scatter | solution.py:113
  164.1 2.3 fusion.34
  166.5 1.6 collective-permute-start.3
  168.1 4.7 constant_dynamic-slice_fusion.2
  172.8 3.1 constant_dynamic-update-slice_fusion.2
  175.9 0.7 pad_maximum_fusion.4
  176.7 0.6 collective-permute-done.3
  177.4 0.8 pad_maximum_fusion.3
  178.1 48.8 %all-gather.6.cloned.1.call-done = bf16[1024,1024]{1,0:T(8,128)(2,1)} async-done(((bf16[128,1024]{1,0:T(8,128)(2,1)}), bf16[1024,1024]{1,0:T(8,128)(2,1)}) %all-gather.6.cloned.1.call-update) | async-done | bytes 2097168 | tf_op jit(solution)/shard_map/all_gather | solution.py:142
  227.2 5.9 multiply_convert_fusion.9
  233.1 1.5 collective-permute-start.5
  234.7 0.8 pad_maximum_fusion.1
  235.6 44.1 %collective-permute-done.5 = bf16[1024,1024]{1,0:T(8,128)(2,1)} collective-permute-done((bf16[1024,1024]{1,0:T(8,128)(2,1)}, bf16[1024,1024]{1,0:T(8,128)(2,1)}, u32[]{:S(2)}, u32[]{:S(2)}) %collective-permute-start.5) | collective-permute-done | bytes 2097184 | tf_op jit(solution)/shard_map/ppermute | solution.py:39
  279.7 8.9 %all-gather.8.cloned.1.call-done = bf16[1024,1536]{1,0:T(8,128)(2,1)} async-done(((bf16[128,1536]{1,0:T(8,128)(2,1)}), bf16[1024,1536]{1,0:T(8,128)(2,1)}) %all-gather.8.cloned.1.call-update) | async-done | bytes 3145744 | tf_op jit(solution)/shard_map/all_gather | solution.py:142
  288.7 7.8 %multiply_convert_fusion.4 = bf16[1024,1536]{1,0:T(8,128)(2,1)} fusion(bf16[1024,1024]{1,0:T(8,128)(2,1)} %get-tuple-element.26, bf16[1024,1536]{1,0:T(8,128)(2,1)} %all-gather.8.cloned.1.call-done), kind=kOutput, calls=%fused_computation.7 | convolution fusion | flops 3224371200 | bytes 8388608 | tf_op jit(solution)/shard_map/dot_general | solution.py:17
  296.5 1.5 collective-permute-start.6
  298.0 0.8 pad_maximum_fusion.2
  298.8 63.8 %all-gather.10.cloned.1.call-done = bf16[1024,2048]{1,0:T(8,128)(2,1)} async-done(((bf16[128,2048]{1,0:T(8,128)(2,1)}), bf16[1024,2048]{1,0:T(8,128)(2,1)}) %all-gather.10.cloned.1.call-update) | async-done | bytes 4194320 | tf_op jit(solution)/shard_map/all_gather | solution.py:142
  362.7 8.3 %multiply_convert_fusion.3 = bf16[1024,2048]{1,0:T(8,128)(2,1)} fusion(bf16[1024,1024]{1,0:T(8,128)(2,1)S(1)} %copy-done.3, bf16[1024,2048]{1,0:T(8,128)(2,1)} %all-gather.10.cloned.1.call-done), kind=kOutput, calls=%fused_computation.5 | convolution fusion | flops 4299161600 | bytes 10485760 | tf_op jit(solution)/shard_map/dot_general | solution.py:17
  371.1 1.0 pad_maximum_fusion
  372.0 7.7 %fusion.18 = f32[1024,2048]{1,0:T(8,128)} fusion(bf16[2048,3328]{1,0:T(8,128)(2,1)} %param.14, bf16[1024,1024]{1,0:T(8,128)(2,1)} %all-gather.6.cloned.1.call-done), kind=kOutput, calls=%fused_computation.49 | convolution fusion | flops 2147483648 | bytes 11534336 | tf_op jit(solution)/shard_map/dot_general | solution.py:11
  379.7 7.4 %fusion.20 = f32[1024,2048]{1,0:T(8,128)} fusion(bf16[2048,3328]{1,0:T(8,128)(2,1)} %param.13, bf16[1024,1024]{1,0:T(8,128)(2,1)S(1)} %copy-done.16), kind=kOutput, calls=%fused_computation.51 | convolution fusion | flops 2147483648 | bytes 11534336 | tf_op jit(solution)/shard_map/dot_general | solution.py:11
  387.1 1.5 collective-permute-start.8
  388.6 2.5 add_convert_fusion.9
  391.1 8.0 %fusion.10 = f32[1024,2048]{1,0:T(8,128)} fusion(bf16[2048,3328]{1,0:T(8,128)(2,1)} %param.14, bf16[1024,1536]{1,0:T(8,128)(2,1)S(1)} %copy-done.14), kind=kOutput, calls=%fused_computation.32 | convolution fusion | flops 3221225472 | bytes 13107200 | tf_op jit(solution)/shard_map/dot_general | solution.py:11
  399.1 7.6 %fusion.12 = f32[1024,2048]{1,0:T(8,128)} fusion(bf16[2048,3328]{1,0:T(8,128)(2,1)} %param.13, bf16[1024,1536]{1,0:T(8,128)(2,1)S(1)} %copy-done.14), kind=kOutput, calls=%fused_computation.34 | convolution fusion | flops 3221225472 | bytes 13107200 | tf_op jit(solution)/shard_map/dot_general | solution.py:11
  406.7 36.1 %all-gather.12.cloned.1.call-done = bf16[1024,2048]{1,0:T(8,128)(2,1)} async-done(((bf16[128,2048]{1,0:T(8,128)(2,1)}), bf16[1024,2048]{1,0:T(8,128)(2,1)}) %all-gather.12.cloned.1.call-update) | async-done | bytes 4194320 | tf_op jit(solution)/shard_map/all_gather | solution.py:142
  442.8 2.8 add_convert_fusion.10
  445.7 3.3 dynamic_update_slice.48
  449.0 3.9 dynamic_update_slice.52
  452.9 0.7 copy-done.7
  453.7 9.1 %fusion.4 = f32[1024,2048]{1,0:T(8,128)} fusion(bf16[2048,3328]{1,0:T(8,128)(2,1)} %param.14, bf16[1024,2048]{1,0:T(8,128)(2,1)S(1)} %copy-done.7), kind=kOutput, calls=%fused_computation.21 | convolution fusion | flops 4294967296 | bytes 14680064 | tf_op jit(solution)/shard_map/dot_general | solution.py:11
  462.8 6.3 %multiply_convert_fusion.2 = bf16[1024,2048]{1,0:T(8,128)(2,1)} fusion(bf16[1024,1024]{1,0:T(8,128)(2,1)S(1)} %copy-done.4, bf16[1024,2048]{1,0:T(8,128)(2,1)S(1)} %copy-done.12), kind=kOutput, calls=%fused_computation.3 | convolution fusion | flops 4299161600 | bytes 10485760 | tf_op jit(solution)/shard_map/dot_general | solution.py:17
  469.1 9.5 %collective-permute-done.8 = bf16[1024,2048]{1,0:T(8,128)(2,1)} collective-permute-done((bf16[1024,2048]{1,0:T(8,128)(2,1)}, bf16[1024,2048]{1,0:T(8,128)(2,1)}, u32[]{:S(2)}, u32[]{:S(2)}) %collective-permute-start.8) | collective-permute-done | bytes 4194336 | tf_op jit(solution)/shard_map/ppermute | solution.py:39
  478.6 1.6 collective-permute-start.9
  480.1 9.1 %fusion = f32[1024,2048]{1,0:T(8,128)} fusion(bf16[2048,3328]{1,0:T(8,128)(2,1)} %param.14, bf16[1024,2048]{1,0:T(8,128)(2,1)S(1)} %copy-done.12), kind=kOutput, calls=%fused_computation.17 | convolution fusion | flops 4294967296 | bytes 14680064 | tf_op jit(solution)/shard_map/dot_general | solution.py:11
  489.2 9.1 %fusion.2 = f32[1024,2048]{1,0:T(8,128)} fusion(bf16[2048,3328]{1,0:T(8,128)(2,1)} %param.13, bf16[1024,2048]{1,0:T(8,128)(2,1)S(1)} %copy-done.12), kind=kOutput, calls=%fused_computation.19 | convolution fusion | flops 4294967296 | bytes 14680064 | tf_op jit(solution)/shard_map/dot_general | solution.py:11
  498.4 24.3 %add_convert_fusion.1 = bf16[1024,2048]{1,0:T(8,128)(2,1)} fusion(f32[1024,2048]{1,0:T(8,128)} %fusion.2, f32[1024,2048]{1,0:T(8,128)} %fusion, f32[1024,2048]{1,0:T(8,128)} %fusion.4, f32[1024,2048]{1,0:T(8,128)} %fusion.12, f32[1024,2048]{1,0:T(8,128)} %fusion.10, f32[1024,2048]{1,0:T(8,128)} %fusion.20, f32[1024,2048]{1,0:T(8,128)} %fusion.18, ...), kind=kOutput, calls=%fused_computation.4 | convolution fusion | flops 4311744512 | bytes 69206016 | tf_op jit(solution)/shard_map/dot_general | solution.py:11
  522.7 1.9 constant_dynamic-slice_fusion
  524.6 0.5 copy-done.15
  525.2 4.5 fusion.39
  529.7 4.6 fusion.40
  534.3 5.4 fusion.14
  539.6 5.5 fusion.16
  545.2 2.1 add_convert_fusion.6
  547.3 21.8 %collective-permute-done.9 = bf16[1024,2048]{1,0:T(8,128)(2,1)} collective-permute-done((bf16[1024,2048]{1,0:T(8,128)(2,1)}, bf16[1024,2048]{1,0:T(8,128)(2,1)}, u32[]{:S(2)}, u32[]{:S(2)}) %collective-permute-start.9) | collective-permute-done | bytes 4194336 | tf_op jit(solution)/shard_map/ppermute | solution.py:39
  569.1 5.4 fusion.15
  574.5 5.6 fusion.17
  580.1 10.3 %multiply_convert_fusion.1 = bf16[1664,2048]{1,0:T(8,128)(2,1)S(1)} fusion(bf16[1024,2048]{1,0:T(8,128)(2,1)} %copy-done.1, bf16[1024,3328]{1,0:T(8,128)(2,1)} %all-gather.14.cloned.1.call-done), kind=kOutput, calls=%fused_computation.2 | convolution fusion | flops 6986137600 | bytes 14417920 | tf_op jit(solution)/shard_map/dot_general | solution.py:17
  590.4 12.9 %add_convert_fusion = bf16[1664,2048]{1,0:T(8,128)(2,1)} fusion(bf16[1664,2048]{1,0:T(8,128)(2,1)S(1)} %multiply_convert_fusion.1, bf16[1024,2048]{1,0:T(8,128)(2,1)} %constant_dynamic-update-slice_fusion.2, bf16[1024,3328]{1,0:T(8,128)(2,1)S(1)} %copy-done.11), kind=kOutput, calls=%fused_computation | convolution fusion | flops 6999769088 | bytes 21233664 | tf_op jit(solution)/shard_map/dot_general | solution.py:17
  (66 shorter events, 1.5 us)
Async XLA Ops:
  7.2 1.6 copy-start.5
  7.2 156.9 %reduce-scatter.2.cloned.1.call-start = ((), (), s32[]{:S(2)}) async-start(), calls=%async_computation.1 | async-start | bytes 7667712 | tf_op jit(solution)/shard_map/reduce_scatter | solution.py:113
  7.2 4.6 collective-permute-start
  13.7 2.0 copy-start.1
  35.9 3.0 copy-start.17
  35.9 3.2 copy-start.18
  36.0 190.9 %all-gather.6.cloned.1.call-start = ((), (), s32[]{:S(2)}) async-start(), calls=%async_computation.2 | async-start | bytes 2359296 | tf_op jit(solution)/shard_map/all_gather | solution.py:142
  36.0 49.0 %collective-permute-start.1 = (bf16[512,2048]{1,0:T(8,128)(2,1)S(1)}, bf16[512,2048]{1,0:T(8,128)(2,1)}, u32[]{:S(2)}, u32[]{:S(2)}) collective-permute-start(bf16[512,2048]{1,0:T(8,128)(2,1)S(1)} %copy-done.5), channel_id=1, source_target_pairs={{0,16},{16,0},{1,17},{17,1},{2,18},{18,2},{3,19},{19,3},{4,20},{20... | collective-permute-start | bytes 6291464 | tf_op jit(solution)/shard_map/ppermute | solution.py:39
  39.0 52.0 %collective-permute-start.4 = (bf16[512,2048]{1,0:T(8,128)(2,1)}, bf16[512,2048]{1,0:T(8,128)(2,1)}, u32[]{:S(2)}, u32[]{:S(2)}) collective-permute-start(bf16[512,2048]{1,0:T(8,128)(2,1)} %param.9), channel_id=1, source_target_pairs={{0,8},{8,0},{1,9},{9,1},{2,10},{10,2},{3,11},{11,3},{4,12},{12,4},... | collective-permute-start | bytes 6291464 | tf_op jit(solution)/shard_map/ppermute | solution.py:39
  39.0 2.8 copy-start.6
  85.0 87.8 %collective-permute-start.2 = (bf16[512,2048]{1,0:T(8,128)(2,1)}, bf16[512,2048]{1,0:T(8,128)(2,1)}, u32[]{:S(2)}, u32[]{:S(2)}) collective-permute-start(bf16[512,2048]{1,0:T(8,128)(2,1)} %collective-permute-done.1), channel_id=1, source_target_pairs={{0,8},{8,0},{1,9},{9,1},{2,10},{10,2},{3,11},{11,3},{4,12},{12,4},... | collective-permute-start | bytes 6291464 | tf_op jit(solution)/shard_map/ppermute | solution.py:39
  87.5 76.5 %copy-start.9 = (bf16[128,3328]{1,0:T(8,128)(2,1)S(1)}, bf16[128,3328]{1,0:T(8,128)(2,1)}, u32[]{:S(2)}) copy-start(bf16[128,3328]{1,0:T(8,128)(2,1)} %param.12) | copy-start | bytes 2555908
  87.5 76.5 %copy-start.10 = (bf16[128,3328]{1,0:T(8,128)(2,1)S(1)}, bf16[128,3328]{1,0:T(8,128)(2,1)}, u32[]{:S(2)}) copy-start(bf16[128,3328]{1,0:T(8,128)(2,1)} %param.11) | copy-start | bytes 2555908
  166.5 10.8 %collective-permute-start.3 = (bf16[128,1664]{1,0:T(8,128)(2,1)S(1)}, bf16[128,1664]{1,0:T(8,128)(2,1)S(1)}, u32[]{:S(2)}, u32[]{:S(2)}) collective-permute-start(bf16[128,1664]{1,0:T(8,128)(2,1)S(1)} %get-tuple-element.52), channel_id=1, source_target_pairs={{0,16},{16,0},{1,17},{17,1},{2,18},{18,2},{3,19},{19,3},{4,20},{20... | collective-permute-start | bytes 1277960 | tf_op jit(solution)/shard_map/ppermute | solution.py:39
  177.3 111.4 %all-gather.8.cloned.1.call-start = ((), (), s32[]{:S(2)}) async-start(), calls=%async_computation.3 | async-start | bytes 3538944 | tf_op jit(solution)/shard_map/all_gather | solution.py:142
  226.9 135.7 %all-gather.10.cloned.1.call-start = ((), (), s32[]{:S(2)}) async-start(), calls=%async_computation.4 | async-start | bytes 4718592 | tf_op jit(solution)/shard_map/all_gather | solution.py:142
  233.1 46.6 %collective-permute-start.5 = (bf16[1024,1024]{1,0:T(8,128)(2,1)}, bf16[1024,1024]{1,0:T(8,128)(2,1)}, u32[]{:S(2)}, u32[]{:S(2)}) collective-permute-start(bf16[1024,1024]{1,0:T(8,128)(2,1)} %multiply_convert_fusion.9), channel_id=1, source_target_pairs={{0,16},{16,0},{1,17},{17,1},{2,18},{18,2},{3,19},{19,3},{4,20},{20... | collective-permute-start | bytes 6291464 | tf_op jit(solution)/shard_map/ppermute | solution.py:39
  288.6 74.0 %copy-start.3 = (bf16[1024,1024]{1,0:T(8,128)(2,1)S(1)}, bf16[1024,1024]{1,0:T(8,128)(2,1)}, u32[]{:S(2)}) copy-start(bf16[1024,1024]{1,0:T(8,128)(2,1)} %get-tuple-element.26) | copy-start | bytes 6291460
  288.7 154.2 %all-gather.12.cloned.1.call-start = ((), (), s32[]{:S(2)}) async-start(), calls=%async_computation.5 | async-start | bytes 4718592 | tf_op jit(solution)/shard_map/all_gather | solution.py:142
  296.5 74.5 %collective-permute-start.6 = (bf16[1024,1536]{1,0:T(8,128)(2,1)}, bf16[1024,1536]{1,0:T(8,128)(2,1)}, u32[]{:S(2)}, u32[]{:S(2)}) collective-permute-start(bf16[1024,1536]{1,0:T(8,128)(2,1)} %multiply_convert_fusion.4), channel_id=1, source_target_pairs={{0,16},{16,0},{1,17},{17,1},{2,18},{18,2},{3,19},{19,3},{4,20},{20... | collective-permute-start | bytes 9437192 | tf_op jit(solution)/shard_map/ppermute | solution.py:39
  371.0 209.1 %all-gather.14.cloned.1.call-start = ((), (), s32[]{:S(2)}) async-start(), calls=%async_computation.6 | async-start | bytes 7667712 | tf_op jit(solution)/shard_map/all_gather | solution.py:151
  372.0 7.7 %copy-start.16 = (bf16[1024,1024]{1,0:T(8,128)(2,1)S(1)}, bf16[1024,1024]{1,0:T(8,128)(2,1)}, u32[]{:S(2)}) copy-start(bf16[1024,1024]{1,0:T(8,128)(2,1)} %all-gather.6.cloned.1.call-done) | copy-start | bytes 6291460
  379.7 8.9 %copy-start.2 = (bf16[1024,1024]{1,0:T(8,128)(2,1)S(1)}, bf16[1024,1024]{1,0:T(8,128)(2,1)}, u32[]{:S(2)}) copy-start(bf16[1024,1024]{1,0:T(8,128)(2,1)} %get-tuple-element.34) | copy-start | bytes 6291460
  387.1 4.0 copy-start.14
  387.1 91.5 %collective-permute-start.8 = (bf16[1024,2048]{1,0:T(8,128)(2,1)}, bf16[1024,2048]{1,0:T(8,128)(2,1)}, u32[]{:S(2)}, u32[]{:S(2)}) collective-permute-start(bf16[1024,2048]{1,0:T(8,128)(2,1)} %multiply_convert_fusion.3), channel_id=1, source_target_pairs={{0,16},{16,0},{1,17},{17,1},{2,18},{18,2},{3,19},{19,3},{4,20},{20... | collective-permute-start | bytes 12582920 | tf_op jit(solution)/shard_map/ppermute | solution.py:39
  449.0 4.7 copy-start.7
  453.7 9.1 %copy-start.4 = (bf16[1024,1024]{1,0:T(8,128)(2,1)S(1)}, bf16[1024,1024]{1,0:T(8,128)(2,1)}, u32[]{:S(2)}) copy-start(bf16[1024,1024]{1,0:T(8,128)(2,1)} %get-tuple-element.26) | copy-start | bytes 6291460
  453.7 9.1 %copy-start.12 = (bf16[1024,2048]{1,0:T(8,128)(2,1)S(1)}, bf16[1024,2048]{1,0:T(8,128)(2,1)}, u32[]{:S(2)}) copy-start(bf16[1024,2048]{1,0:T(8,128)(2,1)} %all-gather.12.cloned.1.call-done) | copy-start | bytes 12582916
  478.6 90.6 %collective-permute-start.9 = (bf16[1024,2048]{1,0:T(8,128)(2,1)}, bf16[1024,2048]{1,0:T(8,128)(2,1)}, u32[]{:S(2)}, u32[]{:S(2)}) collective-permute-start(bf16[1024,2048]{1,0:T(8,128)(2,1)} %multiply_convert_fusion.2), channel_id=1, source_target_pairs={{0,16},{16,0},{1,17},{17,1},{2,18},{18,2},{3,19},{19,3},{4,20},{20... | collective-permute-start | bytes 12582920 | tf_op jit(solution)/shard_map/ppermute | solution.py:39
  522.7 2.5 copy-start.15
  524.6 20.6 %collective-permute-start.7 = (bf16[512,2048]{1,0:T(8,128)(2,1)S(1)}, bf16[512,2048]{1,0:T(8,128)(2,1)S(1)}, u32[]{:S(2)}, u32[]{:S(2)}) collective-permute-start(bf16[512,2048]{1,0:T(8,128)(2,1)S(1)} %constant_dynamic-slice_fusion), channel_id=1, source_target_pairs={{0,8},{8,0},{1,9},{9,1},{2,10},{10,2},{3,11},{11,3},{4,12},{12,4},... | collective-permute-start | bytes 6291464 | tf_op jit(solution)/shard_map/ppermute | solution.py:39
  529.6 4.6 copy-start.8
  539.6 5.5 copy-start
  545.2 24.0 %copy-start.13 = (bf16[1024,2048]{1,0:T(8,128)(2,1)S(1)}, bf16[1024,2048]{1,0:T(8,128)(2,1)}, u32[]{:S(2)}) copy-start(bf16[1024,2048]{1,0:T(8,128)(2,1)} %all-gather.12.cloned.1.call-done) | copy-start | bytes 12582916
  580.1 10.3 %copy-start.11 = (bf16[1024,3328]{1,0:T(8,128)(2,1)S(1)}, bf16[1024,3328]{1,0:T(8,128)(2,1)}, u32[]{:S(2)}) copy-start(bf16[1024,3328]{1,0:T(8,128)(2,1)} %all-gather.14.cloned.1.call-done) | copy-start | bytes 20447236
Sparse Core Ops, SparseCore 0:
  36.1 127.9 reduce-scatter.1
  177.4 49.4 all-gather.5
  229.7 58.9 all-gather.7
  290.6 72.0 all-gather.9
  371.1 71.6 all-gather.11
  444.9 103.8 all-gather.13
